TPU v7x, 32 devices: a whole 2x2x4 slice. The times are simulated.
32 devices in a mesh: rep: 2 (over x), dp: 8 (over z, y), tensor: 2 (over core).
Axes of the slice: x: 2, y: 2, z: 4, core: 2. Of those that a mesh axis runs over, the one named last changes fastest.
Arguments:
- normed_hidden_state: bfloat16 [1024, 8192], P(('rep', 'dp'), 'tensor'), parts along dimension 0, may hold values from -6 to 6
- queries: bfloat16 [1024, 2, 4096], P(('rep', 'dp'), None, 'tensor'), parts along dimension 0
- key_value_cache: bfloat16 [1024, 2, 128, 512], P(('rep', 'dp'), None, None, 'tensor'), parts along dimension 0
- base_projection_weight: bfloat16 [8192, 2, 512], P('tensor'), may hold values from -0.0625 to 0.0625
- adapter_down_weight: bfloat16 [8, 8192, 128], P('dp', 'tensor'), may hold values from -0.0625 to 0.0625
- adapter_up_weight: bfloat16 [8, 2, 64, 512], P('dp', None, None, 'tensor'), may hold values from -0.75 to 0.75
- adapter_index_rows: int32 [1024, 1], P(('rep', 'dp')), parts along dimension 0, may hold values from 0 to 7; in each aligned block of 64 rows (0 to 63, 64 to 127, ...) at most 16 rows name the same one
- placement: int32 [8], replicated, may hold values from 0 to 7, each once
- lengths: int32 [1024], P(('rep', 'dp')), parts along dimension 0, may hold values from 2 to 128, as said below
Outputs:
- attention_out: bfloat16 [1024, 2, 4096], P(('rep', 'dp'), None, 'tensor'), parts along dimension 0
- new_kv: bfloat16 [1024, 2, 512], P(('rep', 'dp'), None, 'tensor'), parts along dimension 0
There are 2 independent parts, one for each index of `rep`. A program takes and returns all parts, laid end to end along the dimension named above; an argument that names none is the same for every part. Nothing has to cross between parts.
Inputs may be any that keep to these rules, and one draw needn't show every extreme that they name: `adapter_index_rows`: in the rows of one index of dp, no adapter is named by more than 16 rows, a bound that some block reaches. `placement`: each adapter has one slot. `lengths`: every 16th row has all 128 slots filled.
All inputs are finite; a program needn't handle non-finite values.
Results may differ from a plain program's by a relative error of at most 0.0054.
Values may be sent and summed in bfloat16 or wider, within the bound.
A program may use at most 128 MiB of HBM per device.

v0:
```python
import jax
import jax.numpy as jnp
from jax import lax
from jax.sharding import PartitionSpec as P

HEAD_SIZE = 128


def attend(queries, key_value_cache, new_kv, lengths):
    rows = queries.shape[0]
    groups = key_value_cache.shape[3] // HEAD_SIZE
    per_group = queries.shape[2] // (HEAD_SIZE * groups)
    query = queries.reshape(rows, 2, groups, per_group, HEAD_SIZE)
    keys = key_value_cache[:, 0].reshape(rows, -1, groups, HEAD_SIZE)
    values = key_value_cache[:, 1].reshape(rows, -1, groups, HEAD_SIZE)
    new_key = new_kv[:, 0, :].reshape(rows, groups, HEAD_SIZE)
    new_value = new_kv[:, 1, :].astype(jnp.float32).reshape(rows, groups, HEAD_SIZE)
    scale = HEAD_SIZE ** (-0.5)
    old_scores = (
        jnp.einsum("rlgqh,rpgh->rlgqp", query, keys, preferred_element_type=jnp.float32) * scale
    )
    positions = jnp.arange(key_value_cache.shape[2], dtype=jnp.int32)
    valid = positions[None, :] < lengths[:, None]
    old_scores = jnp.where(valid[:, None, None, None, :], old_scores, -1e30)
    new_scores = (
        jnp.einsum("rlgqh,rgh->rlgq", query, new_key, preferred_element_type=jnp.float32) * scale
    )
    top = jnp.maximum(jnp.max(old_scores, axis=-1), new_scores)
    old_weights = jnp.exp(old_scores - top[..., None])
    new_weights = jnp.exp(new_scores - top)
    total = jnp.sum(old_weights, axis=-1) + new_weights
    old_probs = (old_weights / total[..., None]).astype(jnp.bfloat16)
    new_probs = (new_weights / total).astype(jnp.bfloat16).astype(jnp.float32)
    mixed = jnp.einsum("rlgqp,rpgh->rlgqh", old_probs, values, preferred_element_type=jnp.float32)
    mixed = mixed + new_probs[..., None] * new_value[:, None, :, None, :]
    return mixed.astype(jnp.bfloat16).reshape(rows, 2, -1)


def per_device(
    normed_hidden_state,
    queries,
    key_value_cache,
    base_projection_weight,
    adapter_down_weight,
    adapter_up_weight,
    adapter_index_rows,
    placement,
    lengths,
):
    rows = normed_hidden_state.shape[0]
    catalog = placement.shape[0]
    matches = adapter_index_rows[:, 0][:, None] == jnp.arange(catalog, dtype=jnp.int32)[None, :]
    slots = jnp.sum(jnp.where(matches, placement[None, :], 0), axis=1)
    partial_value = jnp.dot(
        normed_hidden_state,
        base_projection_weight.reshape(base_projection_weight.shape[0], -1),
        preferred_element_type=jnp.float32,
    ).reshape(rows, 2, -1)
    holders = lax.axis_size("dp")
    capacity = max(2, 2 * rows // holders)
    owners = (slots[:, None] == jnp.arange(holders, dtype=jnp.int32)[None, :]).astype(jnp.int32)
    before = jnp.cumsum(owners, axis=0) - owners
    order = jnp.sum(before * owners, axis=1)
    target = slots * capacity + order
    placing = target[:, None] == jnp.arange(holders * capacity, dtype=jnp.int32)[None, :]
    outgoing = jnp.einsum(
        "rs,rd->sd",
        placing.astype(jnp.bfloat16),
        normed_hidden_state,
        preferred_element_type=jnp.float32,
    )
    outgoing = outgoing.astype(jnp.bfloat16).reshape(holders, capacity, -1)
    whole_up_weight = adapter_up_weight[0]
    up_float = whole_up_weight.astype(jnp.float32)
    middle = jnp.einsum(
        "sid,dk->sik",
        lax.all_to_all(outgoing, "dp", split_axis=0, concat_axis=0, tiled=True),
        adapter_down_weight[0],
        preferred_element_type=jnp.float32,
    )
    middle = lax.psum(middle, "tensor")
    split = middle.reshape(middle.shape[0], middle.shape[1], 2, -1)
    answers = jnp.einsum("siqk,qkc->siqc", split, up_float, precision=lax.Precision.HIGHEST)
    returned = lax.all_to_all(answers, "dp", split_axis=0, concat_axis=0, tiled=True)
    flat = returned.reshape(holders * capacity, 2, -1)
    delta = jnp.einsum(
        "rs,sqc->rqc", placing.astype(jnp.float32), flat, precision=lax.Precision.HIGHEST
    )
    projected = lax.psum_scatter(partial_value, "tensor", scatter_dimension=2, tiled=True) + delta
    new_kv = projected.astype(jnp.bfloat16)
    return (attend(queries, key_value_cache, new_kv, lengths), new_kv)


def solution(mesh):
    placed = (
        P(("rep", "dp"), "tensor"),
        P(("rep", "dp"), None, "tensor"),
        P(("rep", "dp"), None, None, "tensor"),
        P("tensor", None, None),
        P("dp", "tensor", None),
        P("dp", None, None, "tensor"),
        P(("rep", "dp"), None),
        P(),
        P(("rep", "dp")),
    )
    return jax.shard_map(
        per_device,
        mesh=mesh,
        in_specs=placed,
        out_specs=(P(("rep", "dp"), None, "tensor"), P(("rep", "dp"), None, "tensor")),
        check_vma=False,
    )
```

profile of v0, /device:TPU:0, one launch (start us, length us, event | category | flops | bytes accessed | tf_op | source)
XLA Modules:
  0.0 105.1 jit_solution(9864590605722335537)
XLA Ops:
  7.2 0.9 select_reduce_fusion.1
  8.2 0.1 reduce_window_sum.11
  8.3 0.2 select_reduce_fusion
  8.5 2.6 %convolution_convert_fusion = bf16[128,4096]{1,0:T(8,128)(2,1)} fusion(bf16[64,4096]{1,0:T(8,128)(2,1)} %param.9, s32[64]{0:T(128)S(1)} %multiply_add_fusion), kind=kOutput, calls=%fused_computation | convolution fusion | flops 67641344 | bytes 1573120 | tf_op jit(solution)/shard_map/rs,rd->sd/dot_general | solution.py:66
  11.1 7.3 %all-to-all-start = ((bf16[8,16,4096]{2,1,0:T(8,128)(2,1)}), bf16[8,16,4096]{2,1,0:T(8,128)(2,1)S(1)}, u32[]{:S(2)}, u32[]{:S(2)}) async-start(bf16[8,16,4096]{2,1,0:T(8,128)(2,1)} %bitcast.8), calls=%async_computation.1 | async-start | bytes 2097152 | tf_op jit(solution)/shard_map/all_to_all | solution.py:77
  18.4 9.3 %copy.82 = bf16[512,8,2,512]{3,1,2,0:T(8,128)(2,1)} copy(bf16[512,8,2,512]{3,2,1,0:T(2,128)(2,1)} %bitcast.92) | data formatting | bytes 16777216
  27.7 11.3 %copy.55 = bf16[1024,4096]{1,0:T(8,128)(2,1)} copy(bf16[1024,4096]{0,1:T(8,128)(2,1)} %bitcast.90) | data formatting | bytes 16777216 | tf_op jit(solution)/shard_map/dot_general | solution.py:54
  39.0 5.1 %all-to-all-done = bf16[8,16,4096]{2,1,0:T(8,128)(2,1)S(1)} async-done(((bf16[8,16,4096]{2,1,0:T(8,128)(2,1)}), bf16[8,16,4096]{2,1,0:T(8,128)(2,1)S(1)}, u32[]{:S(2)}, u32[]{:S(2)}) %all-to-all-start) | async-done | bytes 1048608 | tf_op jit(solution)/shard_map/all_to_all | solution.py:77
  44.1 0.4 fusion.5
  44.6 0.1 reshape.62
  44.7 0.6 copy.56
  45.4 6.7 %fusion.8 = f32[64,2,512]{2,0,1:T(8,128)} fusion(bf16[2,512,4096]{2,1,0:T(8,128)(2,1)} %bitcast.89, bf16[64,4096]{1,0:T(8,128)(2,1)S(1)} %copy-done.1), kind=kOutput, calls=%fused_computation.15 | convolution fusion | flops 536870912 | bytes 9175040 | tf_op jit(solution)/shard_map/dot_general | solution.py:54
  52.2 6.0 %fusion.24 = (bf16[64,1,128,256]{3,2,1,0:T(8,128)(2,1)}, bf16[64,1,128,256]{3,2,1,0:T(8,128)(2,1)}) fusion(bf16[64,2,128,256]{3,2,1,0:T(8,128)(2,1)} %param.11), kind=kLoop, calls=%fused_computation.42 | loop fusion | bytes 16777216 | tf_op jit(solution)/shard_map/slice | solution.py:14
  58.2 4.2 %all-reduce.2.cloned.1.call-done = f32[8,16,2,64]{3,1,0,2:T(8,128)} async-done(((f32[8,16,2,64]{3,1,0,2:T(8,128)}), f32[8,16,2,64]{3,1,0,2:T(8,128)}) %all-reduce.2.cloned.1.call-update) | async-done | bytes 65552 | tf_op jit(solution)/shard_map/psum | solution.py:81
  62.5 1.2 %convolution_bitcast_fusion.1 = f32[8,16,2,256]{3,1,0,2:T(8,128)S(1)} fusion(f32[8,16,2,64]{3,1,0,2:T(8,128)} %all-reduce.2.cloned.1.call-done, bf16[1,2,64,256]{3,2,1,0:T(8,128)(2,1)S(1)} %copy-done.3), kind=kOutput, calls=%fused_computation.7 | convolution fusion | flops 50331648 | bytes 393216 | tf_op jit(solution)/shard_map/siqk,qkc->siqc/dot_general | solution.py:83
  63.6 0.7 copy.57
  64.3 5.8 %all-to-all-start.1 = ((f32[8,16,2,256]{3,1,2,0:T(8,128)}), f32[8,16,2,256]{3,1,2,0:T(8,128)S(1)}, u32[]{:S(2)}, u32[]{:S(2)}) async-start(f32[8,16,2,256]{3,1,2,0:T(8,128)} %copy.57), calls=%async_computation.2 | async-start | bytes 524288 | tf_op jit(solution)/shard_map/all_to_all | solution.py:84
  70.2 0.3 reshape.59
  70.5 6.4 %copy.80 = bf16[64,1,128,256]{2,3,0,1:T(8,128)(2,1)} copy(bf16[64,1,128,256]{3,2,1,0:T(8,128)(2,1)} %get-tuple-element.12) | data formatting | bytes 8388608
  76.9 3.5 %fusion.26 = (f32[64,2,2,8]{3,1,2,0:T(2,128)S(1)}, f32[64,2,2,8,128]{4,3,1,2,0:T(8,128)S(1)}) fusion(bf16[64,128,2,128,1]{1,3,4,2,0:T(8,128)(2,1)} %bitcast.91, bf16[64,2,2,8,128]{4,3,2,1,0:T(8,128)(2,1)S(1)} %reshape.59, pred[64,128]{1,0:T(8,128)(4,1)S(1)} %iota_compare_fusion.4), kind=kOutput, calls=%fused_computation.44 | convolution fusion | flops 67893248 | bytes 5783552 | tf_op jit(solution)/shard_map/rlgqh,rpgh->rlgqp/dot_general | solution.py:20
  80.5 6.4 %copy.81 = bf16[64,1,128,256]{2,3,0,1:T(8,128)(2,1)} copy(bf16[64,1,128,256]{3,2,1,0:T(8,128)(2,1)} %get-tuple-element.13) | data formatting | bytes 8388608
  87.0 1.2 %fusion.4 = bf16[64,2,256]{2,0,1:T(8,128)(2,1)S(1)} fusion(f32[64,2,256]{2,0,1:T(8,128)} %reduce-scatter.2.cloned.1.call-done, f32[128,2,256]{2,0,1:T(8,128)S(1)} %bitcast.94, s32[64]{0:T(128)S(1)} %multiply_add_fusion), kind=kOutput, calls=%fused_computation.9 | convolution fusion | flops 50405376 | bytes 459008 | tf_op jit(solution)/shard_map/rs,sqc->rqc/dot_general | solution.py:86
  88.1 0.7 copy.68
  88.9 2.4 %fusion.12 = f32[64,2,1,2,8]{4,2,3,1,0:T(1,128)S(1)} fusion(bf16[64,2,128,1,1]{2,3,4,1,0:T(2,128)(2,1)S(1)} %reshape.75, bf16[64,2,2,8,128]{4,3,2,1,0:T(8,128)(2,1)S(1)} %reshape.59), kind=kOutput, calls=%fused_computation.19 | convolution fusion | flops 524288 | bytes 565248 | tf_op jit(solution)/shard_map/rlgqh,rgh->rlgq/dot_general | solution.py:26
  91.3 0.1 copy.72
  91.4 0.2 copy.60
  91.5 0.8 fusion.7
  92.4 0.1 copy.62
  92.6 0.1 copy.65
  92.8 4.5 %fusion.3 = bf16[64,2,2,8,128]{4,3,1,2,0:T(8,128)(2,1)S(1)} fusion(bf16[64,128,2,128,1]{1,3,4,2,0:T(8,128)(2,1)} %bitcast.93, f32[64,2,2,8,128]{4,3,1,2,0:T(8,128)S(1)} %get-tuple-element.19, f32[64,2,128]{2,1,0:T(2,128)S(1)} %reshape.65, f32[64,2,2,8]{3,1,2,0:T(2,128)S(1)} %copy.65, f32[64,2,2,8]{3,1,2,0:T(2,128)S(1)} %copy.62, f32[64,2,2,8]{3,1,2,0:T(2,128)S(1)} %copy.60), kind=kOutput, calls=%fused_computation.6 | convolution fusion | flops 68681728 | bytes 5857280 | tf_op jit(solution)/shard_map/rlgqp,rpgh->rlgqh/dot_general | solution.py:34
  97.3 0.1 copy.78
  97.4 0.9 reshape.76
  (27 shorter events, 0.6 us)
Async XLA Ops:
  7.2 37.0 %copy-start = (bf16[1,4096,128]{2,1,0:T(8,128)(2,1)S(1)}, bf16[1,4096,128]{2,1,0:T(8,128)(2,1)}, u32[]{:S(2)}) copy-start(bf16[1,4096,128]{2,1,0:T(8,128)(2,1)} %param.13) | copy-start | bytes 3145732
  11.1 33.1 %all-to-all-start = ((bf16[8,16,4096]{2,1,0:T(8,128)(2,1)}), bf16[8,16,4096]{2,1,0:T(8,128)(2,1)S(1)}, u32[]{:S(2)}, u32[]{:S(2)}) async-start(bf16[8,16,4096]{2,1,0:T(8,128)(2,1)} %bitcast.8), calls=%async_computation.1 | async-start | bytes 2097152 | tf_op jit(solution)/shard_map/all_to_all | solution.py:77
  18.4 44.1 %all-reduce.2.cloned.1.call-start = ((), (), s32[]{:S(2)}) async-start(), calls=%async_computation.4 | async-start | bytes 262144 | tf_op jit(solution)/shard_map/psum | solution.py:81
  27.7 17.7 %copy-start.1 = (bf16[64,4096]{1,0:T(8,128)(2,1)S(1)}, bf16[64,4096]{1,0:T(8,128)(2,1)}, u32[]{:S(2)}) copy-start(bf16[64,4096]{1,0:T(8,128)(2,1)} %param.9) | copy-start | bytes 1572868
  45.4 41.6 %reduce-scatter.2.cloned.1.call-start = ((), (), s32[]{:S(2)}) async-start(), calls=%async_computation.3 | async-start | bytes 393216 | tf_op jit(solution)/shard_map/reduce_scatter | solution.py:89
  52.2 10.3 %copy-start.3 = (bf16[1,2,64,256]{3,2,1,0:T(8,128)(2,1)S(1)}, bf16[1,2,64,256]{3,2,1,0:T(8,128)(2,1)}, u32[]{:S(2)}) copy-start(bf16[1,2,64,256]{3,2,1,0:T(8,128)(2,1)} %param.14) | copy-start | bytes 196612
  52.2 17.9 %copy-start.4 = (s32[64]{0:T(128)S(1)}, s32[64]{0:T(128)}, u32[]{:S(2)}) copy-start(s32[64]{0:T(128)} %param.17) | copy-start | bytes 772
  52.2 18.0 %copy-start.2 = (bf16[64,2,2048]{2,1,0:T(2,128)(2,1)S(1)}, bf16[64,2,2048]{2,1,0:T(2,128)(2,1)}, u32[]{:S(2)}) copy-start(bf16[64,2,2048]{2,1,0:T(2,128)(2,1)} %param.10) | copy-start | bytes 1572868
  64.3 22.6 %all-to-all-start.1 = ((f32[8,16,2,256]{3,1,2,0:T(8,128)}), f32[8,16,2,256]{3,1,2,0:T(8,128)S(1)}, u32[]{:S(2)}, u32[]{:S(2)}) async-start(f32[8,16,2,256]{3,1,2,0:T(8,128)} %copy.57), calls=%async_computation.2 | async-start | bytes 524288 | tf_op jit(solution)/shard_map/all_to_all | solution.py:84
Sparse Core Ops, SparseCore 0:
  45.5 16.9 all-reduce.1
  65.2 8.8 reduce-scatter.1
where the time goes:
time: 106 us; the launch traced here: 105 us
  local copies, waits for them, and re-layouts  43.7 us (41%)
  matrix products  22.5 us (21%)
  between operations  14.2 us (13%)
  starting transfers between devices  13.1 us (12%)
  waiting for transfers between devices  9.39 us (9%)
  other arithmetic  2.2 us (2%)
    unnamed x16, local copies, waits for them, and re-layouts  23.8 us
    dot_general x1, local copies, waits for them, and re-layouts, per_device(): jnp.dot(normed_hidden_state, base_projection_weight.reshape(base_projecti...  11.3 us
    all_to_all x1, starting transfers between devices, per_device(): lax.all_to_all(outgoing, 'dp', split_axis=0, concat_axis=0, tiled=True)  7.28 us
    dot_general x1, matrix products, per_device(): jnp.dot(normed_hidden_state, base_projection_weight.reshape(base_projecti...  6.74 us
    slice x1, local copies, waits for them, and re-layouts, attend(): keys = key_value_cache[:, 0].reshape(rows, -1, groups, HEAD_SIZE)  5.98 us
    all_to_all x1, starting transfers between devices, per_device(): lax.all_to_all(answers, 'dp', split_axis=0, concat_axis=0, tiled=True)  5.77 us
    all_to_all x1, waiting for transfers between devices, per_device(): lax.all_to_all(outgoing, 'dp', split_axis=0, concat_axis=0, tiled=True)  5.1 us
    dot_general x1, matrix products, attend(): jnp.einsum('rlgqp,rpgh->rlgqh', old_probs, values, preferred_element_type...  4.51 us
  transfers between devices with their start and end apart: 4, of which 2 were waited for; matrix products, arithmetic and copies ran while one was open for 49% of the time, Pallas kernels for 0%

commit v1 on v0

v1 whole, which is shorter than its diff:
```python
import functools

import jax
import jax.numpy as jnp
from jax import lax
from jax.experimental import pallas as pl
from jax.experimental.pallas import tpu as pltpu
from jax.sharding import PartitionSpec as P

HEAD = 128
MESH = pl.DeviceIdType.MESH
BF16 = jnp.bfloat16
F32 = jnp.float32
SLOTS = 16


def iota(shape, dim):
    return lax.broadcasted_iota(jnp.int32, shape, dim)


def kernel(
    n,
    hid_ref,
    idx_ref,
    place_ref,
    len_ref,
    up_ref,
    q_hbm,
    cache_hbm,
    w_hbm,
    d_hbm,
    out_ref,
    kv_ref,
    qbuf,
    cbuf,
    wbuf,
    dbuf,
    sendbuf,
    recvbuf,
    wide,
    back_t,
    base,
    base_in,
    mid,
    mid_in,
    ans,
    ret,
    newkv,
    top,
    total,
    mixed,
    local_sem,
    w_sem,
    out_send,
    out_recv,
    ret_send,
    ret_recv,
    pair_send,
    pair_recv,
):
    rows, width = hid_ref.shape
    tiles = wbuf.shape[0]
    half = tiles // 2
    groups = cbuf.shape[3] // HEAD
    slots = n * SLOTS
    me = lax.axis_index("dp")
    side = lax.axis_index("tensor")
    other = 1 - side
    per_row = qbuf.shape[0] // rows
    per_group = per_row // groups

    loads = [
        pltpu.make_async_copy(q_hbm, qbuf, local_sem.at[0]),
        pltpu.make_async_copy(cache_hbm, cbuf, local_sem.at[1]),
        pltpu.make_async_copy(d_hbm, dbuf, local_sem.at[2]),
    ]
    w_loads = [
        pltpu.make_async_copy(w_hbm.at[:, :, pl.ds(c * 128, 128)], wbuf.at[c], w_sem.at[c])
        for c in range(tiles)
    ]

    barrier = pltpu.get_barrier_semaphore()
    for o in range(1, n):
        pl.semaphore_signal(
            barrier, inc=1, device_id={"dp": lax.rem(me + o, n)}, device_id_type=MESH
        )
    pl.semaphore_signal(barrier, inc=1, device_id={"tensor": other}, device_id_type=MESH)
    for copy in w_loads:
        copy.start()
    for copy in loads:
        copy.start()

    index = idx_ref[...]
    slot = jnp.zeros((1, rows), jnp.int32)
    for a in range(n):
        slot = slot + jnp.where(index == a, place_ref[a], 0)
    slot = slot.astype(F32)
    first, second = iota((rows, rows), 0), iota((rows, rows), 1)
    across = jnp.broadcast_to(slot, (rows, rows))
    down = jnp.sum(jnp.where(first == second, across, 0.0), axis=1, keepdims=True)
    same = jnp.where((down == across) & (first < second), 1.0, 0.0)
    target = slot * SLOTS + jnp.sum(same, axis=0, keepdims=True)
    target_down = jnp.sum(
        jnp.where(first == second, jnp.broadcast_to(target, (rows, rows)), 0.0),
        axis=1,
        keepdims=True,
    )
    placing = jnp.where(iota((slots, rows), 0).astype(F32) == target, 1.0, 0.0).astype(BF16)
    back_t[...] = jnp.where(
        iota((rows, slots), 1).astype(F32) == target_down, 1.0, 0.0
    ).astype(BF16)
    step = 1024
    for c in range(0, width, step):
        sendbuf[:, c : c + step] = jnp.dot(
            placing, hid_ref[:, c : c + step], preferred_element_type=F32
        ).astype(BF16)

    pl.semaphore_wait(barrier, n)
    mine = pl.ds(pl.multiple_of(me * SLOTS, SLOTS), SLOTS)

    def block(d):
        return pl.ds(pl.multiple_of(d * SLOTS, SLOTS), SLOTS)

    order = sorted(range(1, n), key=lambda o: -min(o, n - o))
    dispatch = []
    for o in order:
        d = lax.rem(me + o, n)
        dispatch.append(
            pltpu.make_async_remote_copy(
                src_ref=sendbuf.at[block(d), :],
                dst_ref=recvbuf.at[mine, :],
                send_sem=out_send.at[o],
                recv_sem=out_recv.at[o],
                device_id={"dp": d},
                device_id_type=MESH,
            )
        )
    for copy in dispatch:
        copy.start()
    recvbuf[mine, :] = sendbuf[mine, :]

    deep = 256
    spreads = [
        jnp.where(iota((deep, 2 * deep), 1) == 2 * iota((deep, 2 * deep), 0) + j, 1.0, 0.0).astype(
            BF16
        )
        for j in range(2)
    ]
    gang = 4
    for c in range(0, width, gang * deep):
        stack = jnp.concatenate(
            [hid_ref[:, c + i * deep : c + (i + 1) * deep] for i in range(gang)], axis=0
        )
        for j in range(2):
            res = jnp.dot(stack, spreads[j], preferred_element_type=F32).astype(BF16)
            for i in range(gang):
                at = 2 * (c + i * deep)
                wide[j * rows : (j + 1) * rows, at : at + 2 * deep] = res[
                    i * rows : (i + 1) * rows
                ]
    for copy in w_loads:
        copy.wait()
    chunk = 2048
    for h in range(2):
        acc = jnp.zeros((2 * rows, half * 128), F32)
        for k in range(0, 2 * width, chunk):
            rhs = jnp.concatenate(
                [
                    wbuf.at[h * half + c].reshape(2 * width, 128)[k : k + chunk, :]
                    for c in range(half)
                ],
                axis=1,
            )
            acc = acc + jnp.dot(wide[:, k : k + chunk], rhs, preferred_element_type=F32)
        base[h] = acc
    base_copy = pltpu.make_async_remote_copy(
        src_ref=base.at[other],
        dst_ref=base_in,
        send_sem=pair_send.at[0],
        recv_sem=pair_recv.at[0],
        device_id={"tensor": other},
        device_id_type=MESH,
    )
    base_copy.start()

    for copy in loads:
        copy.wait()
    scale = HEAD ** (-0.5)
    unroll = 4

    def old(i, carry):
        for u in range(unroll):
            r = i * unroll + u
            span = pl.ds(pl.multiple_of(r * per_row, per_row), per_row)
            query = qbuf[span, :]
            blank = jnp.zeros((per_group, HEAD), BF16)
            lhs = jnp.concatenate(
                [
                    jnp.concatenate(
                        [
                            query[g * per_group : (g + 1) * per_group] if g == k else blank
                            for k in range(groups)
                        ],
                        axis=1,
                    )
                    for g in range(groups)
                ],
                axis=0,
            )
            s = (
                lax.dot_general(
                    lhs, cbuf[r, 0], (((1,), (1,)), ((), ())), preferred_element_type=F32
                )
                * scale
            )
            s = jnp.where(iota(s.shape, 1) < len_ref[r], s, -1e30)
            m = jnp.max(s, axis=1, keepdims=True)
            e = jnp.exp(s - m)
            o = jnp.dot(e.astype(BF16), cbuf[r, 1], preferred_element_type=F32)
            top[span, :] = jnp.broadcast_to(m, (per_row, HEAD))
            total[span, :] = jnp.broadcast_to(
                jnp.sum(e, axis=1, keepdims=True), (per_row, HEAD)
            )
            mixed[span, :] = jnp.concatenate(
                [
                    o[g * per_group : (g + 1) * per_group, g * HEAD : (g + 1) * HEAD]
                    for g in range(groups)
                ],
                axis=0,
            )
        return carry

    lax.fori_loop(0, rows // unroll, old, 0)

    for copy in dispatch:
        copy.wait_recv()
    mid[...] = jnp.dot(recvbuf[...], dbuf[...], preferred_element_type=F32)
    mid_copy = pltpu.make_async_remote_copy(
        src_ref=mid,
        dst_ref=mid_in,
        send_sem=pair_send.at[1],
        recv_sem=pair_recv.at[1],
        device_id={"tensor": other},
        device_id_type=MESH,
    )
    mid_copy.start()
    up = up_ref[...]
    none = jnp.zeros(up.shape[1:], BF16)
    up_both = jnp.concatenate(
        [jnp.concatenate([up[0], none], axis=1), jnp.concatenate([none, up[1]], axis=1)], axis=0
    )
    mid_copy.wait_recv()
    middle = mid[...] + mid_in[...]
    high = middle.astype(BF16)
    low = (middle - high.astype(F32)).astype(BF16)
    ans[...] = (
        jnp.dot(high, up_both, preferred_element_type=F32)
        + jnp.dot(low, up_both, preferred_element_type=F32)
    ).astype(BF16)
    returns = []
    for o in order:
        d = lax.rem(me + o, n)
        returns.append(
            pltpu.make_async_remote_copy(
                src_ref=ans.at[block(d), :],
                dst_ref=ret.at[mine, :],
                send_sem=ret_send.at[o],
                recv_sem=ret_recv.at[o],
                device_id={"dp": d},
                device_id_type=MESH,
            )
        )
    for copy in returns:
        copy.start()
    ret[mine, :] = ans[mine, :]
    base_copy.wait_recv()
    for copy in returns:
        copy.wait_recv()
    delta = jnp.dot(back_t[...], ret[...], preferred_element_type=F32)
    own = half * 128
    packed = jnp.zeros((rows * 2 * groups, HEAD), F32)
    for j in range(2):
        part = slice(j * rows, (j + 1) * rows)
        value = base[side, part, :] + base_in[part, :] + delta[:, j * own : (j + 1) * own]
        value = value.astype(BF16)
        newkv[j] = value.astype(F32)
        for g in range(groups):
            shape = (rows * 2 * groups, rows)
            put = jnp.where(
                iota(shape, 0) == 2 * groups * iota(shape, 1) + 2 * g + j, 1.0, 0.0
            ).astype(BF16)
            packed = packed + jnp.dot(
                put, value[:, g * HEAD : (g + 1) * HEAD], preferred_element_type=F32
            )
    kv_ref[...] = packed.astype(BF16)

    many = 8

    def finish(i, carry):
        here = pl.ds(pl.multiple_of(i * many, many), many)
        keys = newkv[0, here, :]
        values = newkv[1, here, :]
        for u in range(many):
            r = i * many + u
            for g in range(groups):
                at = pl.multiple_of(r * per_row + g * per_group, per_group)
                span = pl.ds(at, per_group)
                key = keys[u : u + 1, g * HEAD : (g + 1) * HEAD]
                value = values[u : u + 1, g * HEAD : (g + 1) * HEAD]
                s = jnp.sum(qbuf[span, :].astype(F32) * key, axis=1, keepdims=True) * scale
                was = top[span, :]
                now = jnp.maximum(was, s)
                a = jnp.exp(was - now)
                b = jnp.exp(s - now)
                whole = total[span, :] * a + b
                out_ref[span, :] = ((mixed[span, :] * a + b * value) / whole).astype(BF16)
        return carry

    lax.fori_loop(0, rows // many, finish, 0)
    for copy in dispatch:
        copy.wait_send()
    for copy in returns:
        copy.wait_send()
    base_copy.wait_send()
    mid_copy.wait_send()


def per_device(hid, queries, cache, base_w, down_w, up_w, index, placement, lengths):
    n = lax.axis_size("dp")
    rows, width = hid.shape
    heads = queries.shape[2] // HEAD
    tiles = base_w.shape[2] // 128
    groups = cache.shape[3] // HEAD
    slots = n * SLOTS
    q = queries.reshape(rows, 2, heads, HEAD).transpose(0, 2, 1, 3).reshape(-1, HEAD)
    own = cache.shape[3]
    rank = down_w.shape[2]
    vmem = pl.BlockSpec(memory_space=pltpu.VMEM)
    smem = pl.BlockSpec(memory_space=pltpu.SMEM)
    hbm = pl.BlockSpec(memory_space=pl.ANY)
    out, kv = pl.pallas_call(
        functools.partial(kernel, n),
        out_shape=(
            jax.ShapeDtypeStruct(q.shape, BF16),
            jax.ShapeDtypeStruct((rows * 2 * groups, HEAD), BF16),
        ),
        in_specs=[vmem, vmem, smem, smem, vmem, hbm, hbm, hbm, hbm],
        out_specs=(vmem, vmem),
        scratch_shapes=[
            pltpu.VMEM(q.shape, BF16),
            pltpu.VMEM(cache.shape, BF16),
            pltpu.VMEM((tiles, width, 2, 128), BF16),
            pltpu.VMEM((width, rank), BF16),
            pltpu.VMEM((slots, width), BF16),
            pltpu.VMEM((slots, width), BF16),
            pltpu.VMEM((2 * rows, 2 * width), BF16),
            pltpu.VMEM((rows, slots), BF16),
            pltpu.VMEM((2, 2 * rows, own), F32),
            pltpu.VMEM((2 * rows, own), F32),
            pltpu.VMEM((slots, rank), F32),
            pltpu.VMEM((slots, rank), F32),
            pltpu.VMEM((slots, 2 * own), BF16),
            pltpu.VMEM((slots, 2 * own), BF16),
            pltpu.VMEM((2, rows, own), F32),
            pltpu.VMEM(q.shape, F32),
            pltpu.VMEM(q.shape, F32),
            pltpu.VMEM(q.shape, F32),
            pltpu.SemaphoreType.DMA((3,)),
            pltpu.SemaphoreType.DMA((tiles,)),
            pltpu.SemaphoreType.DMA((n,)),
            pltpu.SemaphoreType.DMA((n,)),
            pltpu.SemaphoreType.DMA((n,)),
            pltpu.SemaphoreType.DMA((n,)),
            pltpu.SemaphoreType.DMA((2,)),
            pltpu.SemaphoreType.DMA((2,)),
        ],
        compiler_params=pltpu.CompilerParams(
            collective_id=0, has_side_effects=True, vmem_limit_bytes=56 * 1024 * 1024
        ),
    )(
        hid,
        index.reshape(1, rows),
        placement,
        lengths,
        up_w[0],
        q,
        cache,
        base_w,
        down_w[0],
    )
    out = out.reshape(rows, heads, 2, HEAD).transpose(0, 2, 1, 3).reshape(rows, 2, -1)
    kv = kv.reshape(rows, groups, 2, HEAD).transpose(0, 2, 1, 3).reshape(rows, 2, -1)
    return out, kv


def solution(mesh):
    placed = (
        P(("rep", "dp"), "tensor"),
        P(("rep", "dp"), None, "tensor"),
        P(("rep", "dp"), None, None, "tensor"),
        P("tensor", None, None),
        P("dp", "tensor", None),
        P("dp", None, None, "tensor"),
        P(("rep", "dp"), None),
        P(),
        P(("rep", "dp")),
    )
    return jax.shard_map(
        per_device,
        mesh=mesh,
        in_specs=placed,
        out_specs=(P(("rep", "dp"), None, "tensor"), P(("rep", "dp"), None, "tensor")),
        check_vma=False,
    )
```

time: 106 us -> 46.3 us (0.44)
  Pallas kernels: 0 us -> 41.7 us
  local copies, waits for them, and re-layouts: 43.7 us -> 3.71 us
  matrix products: 22.5 us -> 0 us
  between operations: 14.2 us -> 0.64 us
  starting transfers between devices: 13.1 us -> 0 us
  waiting for transfers between devices: 9.39 us -> 0 us
  other arithmetic: 2.2 us -> 0 us
    pallas_call x0 -> x1, Pallas kernels: none -> 41.7 us  [per_device(): pl.pallas_call(functools.partial(kernel, n), out_shape=(jax.ShapeDtypeStr...]
    dot_general x8 -> x0, matrix products: 22.5 us -> none  [the longest x1 6.74 us: per_device(): jnp.dot(normed_hidden_state, base_projection_weight.reshape(base_projecti...]
    unnamed x16 -> x2, local copies, waits for them, and re-layouts: 23.8 us -> 3.71 us
    all_to_all x2 -> x0, starting transfers between devices: 13.1 us -> none  [the longest x1 7.28 us: per_device(): lax.all_to_all(outgoing, 'dp', split_axis=0, concat_axis=0, tiled=True)]
    dot_general x2 -> x0, local copies, waits for them, and re-layouts: 11.4 us -> none  [the longest x1 11.3 us: per_device(): jnp.dot(normed_hidden_state, base_projection_weight.reshape(base_projecti...]
    slice x1 -> x0, local copies, waits for them, and re-layouts: 5.98 us -> none  [attend(): keys = key_value_cache[:, 0].reshape(rows, -1, groups, HEAD_SIZE)]
    all_to_all x2 -> x0, waiting for transfers between devices: 5.1 us -> none  [the longest x1 5.1 us: per_device(): lax.all_to_all(outgoing, 'dp', split_axis=0, concat_axis=0, tiled=True)]
    psum x1 -> x0, waiting for transfers between devices: 4.23 us -> none  [per_device(): middle = lax.psum(middle, 'tensor')]
  transfers between devices with their start and end apart: 4 -> 0, of which waited for: 2 -> 0; matrix products, arithmetic and copies ran while one was open for 49% -> 0% of each run, Pallas kernels for 0% -> 0%
where the time goes in v1:
time: 46.3 us; the launch traced here: 46.1 us
  Pallas kernels  41.7 us (90%)
  local copies, waits for them, and re-layouts  3.71 us (8%)
  between operations  0.64 us (1%)
    pallas_call x1, Pallas kernels, per_device(): pl.pallas_call(functools.partial(kernel, n), out_shape=(jax.ShapeDtypeStr...  41.7 us
    unnamed x2, local copies, waits for them, and re-layouts  3.71 us

profile of v1, /device:TPU:0, one launch (start us, length us, event | category | flops | bytes accessed | tf_op | source)
XLA Modules:
  0.0 46.1 jit_solution(17029783335318364806)
XLA Ops:
  0.6 41.7 %shard_map.104 = (bf16[2048,128]{1,0:T(8,128)(2,1)}, bf16[256,128]{1,0:T(8,128)(2,1)}) custom-call(bf16[64,4096]{1,0:T(8,128)(2,1)} %hid_ref.1, s32[1,64]{1,0:T(1,128)} %bitcast.23, s32[8]{0:T(128)} %place_ref.1, s32[64]{0:T(128)} %len_ref.1, bf16[2,64,256]{2,1,0:T(8,128)(2,1)} %bitcast.21, bf16[2048,128]{1,0:T(8,128)(2,1)} %bitcast.19, ...), custom_call_target="tpu_custom_call" | custom-call | tf_op jit(solution)/shard_map/pallas_call | solution.py:341
  42.3 2.2 %copy.16 = bf16[64,2,2048]{2,1,0:T(2,128)(2,1)} copy(bf16[64,2,2048]{2,1,0:T(2,128)(2,1)} %bitcast.20) | data formatting | bytes 1048576
  44.5 1.5 %copy.17 = bf16[64,2,256]{2,1,0:T(2,128)(2,1)} copy(bf16[64,2,256]{2,1,0:T(2,128)(2,1)} %bitcast.22) | data formatting | bytes 131072

commit v2 on v1

--- a/solution.py
+++ b/solution.py
@@ -186,48 +186,54 @@
     for copy in loads:
         copy.wait()
     scale = HEAD ** (-0.5)
-    unroll = 4
+    unroll = 8
+
+    def spread(query):
+        blank = jnp.zeros((per_group, HEAD), BF16)
+        return jnp.concatenate(
+            [
+                jnp.concatenate(
+                    [
+                        query[g * per_group : (g + 1) * per_group] if g == k else blank
+                        for k in range(groups)
+                    ],
+                    axis=1,
+                )
+                for g in range(groups)
+            ],
+            axis=0,
+        )
 
     def old(i, carry):
-        for u in range(unroll):
-            r = i * unroll + u
-            span = pl.ds(pl.multiple_of(r * per_row, per_row), per_row)
-            query = qbuf[span, :]
-            blank = jnp.zeros((per_group, HEAD), BF16)
-            lhs = jnp.concatenate(
-                [
-                    jnp.concatenate(
-                        [
-                            query[g * per_group : (g + 1) * per_group] if g == k else blank
-                            for k in range(groups)
-                        ],
-                        axis=1,
-                    )
-                    for g in range(groups)
-                ],
-                axis=0,
+        members = [i * unroll + u for u in range(unroll)]
+        spans = [pl.ds(pl.multiple_of(r * per_row, per_row), per_row) for r in members]
+        scores = [
+            lax.dot_general(
+                spread(qbuf[span, :]),
+                cbuf[r, 0],
+                (((1,), (1,)), ((), ())),
+                preferred_element_type=F32,
             )
-            s = (
-                lax.dot_general(
-                    lhs, cbuf[r, 0], (((1,), (1,)), ((), ())), preferred_element_type=F32
-                )
-                * scale
-            )
-            s = jnp.where(iota(s.shape, 1) < len_ref[r], s, -1e30)
-            m = jnp.max(s, axis=1, keepdims=True)
-            e = jnp.exp(s - m)
-            o = jnp.dot(e.astype(BF16), cbuf[r, 1], preferred_element_type=F32)
+            for r, span in zip(members, spans)
+        ]
+        scores = [
+            jnp.where(iota(s.shape, 1) < len_ref[r], s * scale, -1e30)
+            for r, s in zip(members, scores)
+        ]
+        tops = [jnp.max(s, axis=1, keepdims=True) for s in scores]
+        weights = [jnp.exp(s - m) for s, m in zip(scores, tops)]
+        outs = [
+            jnp.dot(e.astype(BF16), cbuf[r, 1], preferred_element_type=F32)
+            for r, e in zip(members, weights)
+        ]
+        sums = [jnp.sum(e, axis=1, keepdims=True) for e in weights]
+        for span, m, l, o in zip(spans, tops, sums, outs):
             top[span, :] = jnp.broadcast_to(m, (per_row, HEAD))
-            total[span, :] = jnp.broadcast_to(
-                jnp.sum(e, axis=1, keepdims=True), (per_row, HEAD)
-            )
-            mixed[span, :] = jnp.concatenate(
-                [
-                    o[g * per_group : (g + 1) * per_group, g * HEAD : (g + 1) * HEAD]
-                    for g in range(groups)
-                ],
-                axis=0,
-            )
+            total[span, :] = jnp.broadcast_to(l, (per_row, HEAD))
+            for g in range(groups):
+                part = slice(g * per_group, (g + 1) * per_group)
+                at = pl.ds(pl.multiple_of(span.start + g * per_group, per_group), per_group)
+                mixed[at, :] = o[part, g * HEAD : (g + 1) * HEAD]
         return carry
 
     lax.fori_loop(0, rows // unroll, old, 0)
@@ -323,6 +329,11 @@
         copy.wait_send()
     base_copy.wait_send()
     mid_copy.wait_send()
+
+
+def land(a_ref, b_ref, x_ref, y_ref):
+    x_ref[...] = a_ref[...]
+    y_ref[...] = b_ref[...]
 
 
 def per_device(hid, queries, cache, base_w, down_w, up_w, index, placement, lengths):
@@ -388,6 +399,15 @@
         base_w,
         down_w[0],
     )
+    out, kv = pl.pallas_call(
+        land,
+        out_shape=(
+            jax.ShapeDtypeStruct(out.shape, BF16),
+            jax.ShapeDtypeStruct(kv.shape, BF16),
+        ),
+        in_specs=[vmem, vmem],
+        out_specs=(vmem, vmem),
+    )(out, kv)
     out = out.reshape(rows, heads, 2, HEAD).transpose(0, 2, 1, 3).reshape(rows, 2, -1)
     kv = kv.reshape(rows, groups, 2, HEAD).transpose(0, 2, 1, 3).reshape(rows, 2, -1)
     return out, kv

time: 46.3 us -> 41.6 us (0.90)
  local copies, waits for them, and re-layouts: 3.71 us -> 0 us
  Pallas kernels: 41.7 us -> 40.8 us
    unnamed x2 -> x0, local copies, waits for them, and re-layouts: 3.71 us -> none
    pallas_call x1, Pallas kernels: 41.7 us -> 38.9 us  [per_device(): pl.pallas_call(functools.partial(kernel, n), out_shape=(jax.ShapeDtypeStr...]
    pallas_call x0 -> x1, Pallas kernels: none -> 1.88 us  [per_device(): pl.pallas_call(land, out_shape=(jax.ShapeDtypeStruct(out.shape, BF16), ja...]
where the time goes in v2:
time: 41.6 us; the launch traced here: 41.4 us
  Pallas kernels  40.8 us (98%)
  between operations  0.64 us (2%)
    pallas_call x1, Pallas kernels, per_device(): pl.pallas_call(functools.partial(kernel, n), out_shape=(jax.ShapeDtypeStr...  38.9 us
    pallas_call x1, Pallas kernels, per_device(): pl.pallas_call(land, out_shape=(jax.ShapeDtypeStruct(out.shape, BF16), ja...  1.88 us

profile of v2, /device:TPU:0, one launch (start us, length us, event | category | flops | bytes accessed | tf_op | source)
XLA Modules:
  0.0 41.4 jit_solution(7354354914702027544)
XLA Ops:
  0.6 38.9 %shard_map.104 = (bf16[2048,128]{1,0:T(8,128)(2,1)}, bf16[256,128]{1,0:T(8,128)(2,1)}) custom-call(bf16[64,4096]{1,0:T(8,128)(2,1)} %hid_ref.1, s32[1,64]{1,0:T(1,128)} %bitcast.21, s32[8]{0:T(128)} %place_ref.1, s32[64]{0:T(128)} %len_ref.1, bf16[2,64,256]{2,1,0:T(8,128)(2,1)} %bitcast.20, bf16[2048,128]{1,0:T(8,128)(2,1)} %bitcast.19, ...), custom_call_target="tpu_custom_call" | custom-call | tf_op jit(solution)/shard_map/pallas_call | solution.py:352
  39.5 1.9 %shard_map.105 = (bf16[2048,128]{1,0:T(8,128)(2,1)}, bf16[256,128]{1,0:T(8,128)(2,1)}) custom-call(bf16[2048,128]{1,0:T(8,128)(2,1)} %get-tuple-element.6.a_ref, bf16[256,128]{1,0:T(8,128)(2,1)} %get-tuple-element.7.b_ref), custom_call_target="tpu_custom_call" | custom-call | tf_op jit(solution)/shard_map/pallas_call | solution.py:402

commit v3 on v2

--- a/solution.py
+++ b/solution.py
@@ -306,20 +306,29 @@
         here = pl.ds(pl.multiple_of(i * many, many), many)
         keys = newkv[0, here, :]
         values = newkv[1, here, :]
-        for u in range(many):
-            r = i * many + u
-            for g in range(groups):
-                at = pl.multiple_of(r * per_row + g * per_group, per_group)
-                span = pl.ds(at, per_group)
-                key = keys[u : u + 1, g * HEAD : (g + 1) * HEAD]
-                value = values[u : u + 1, g * HEAD : (g + 1) * HEAD]
-                s = jnp.sum(qbuf[span, :].astype(F32) * key, axis=1, keepdims=True) * scale
-                was = top[span, :]
-                now = jnp.maximum(was, s)
-                a = jnp.exp(was - now)
-                b = jnp.exp(s - now)
-                whole = total[span, :] * a + b
-                out_ref[span, :] = ((mixed[span, :] * a + b * value) / whole).astype(BF16)
+        pairs = [(u, g) for u in range(many) for g in range(groups)]
+        spans = [
+            pl.ds(
+                pl.multiple_of((i * many + u) * per_row + g * per_group, per_group), per_group
+            )
+            for u, g in pairs
+        ]
+        keys = [keys[u : u + 1, g * HEAD : (g + 1) * HEAD] for u, g in pairs]
+        values = [values[u : u + 1, g * HEAD : (g + 1) * HEAD] for u, g in pairs]
+        scores = [
+            jnp.sum(qbuf[span, :].astype(F32) * key, axis=1, keepdims=True) * scale
+            for span, key in zip(spans, keys)
+        ]
+        results = []
+        for span, s, value in zip(spans, scores, values):
+            was = top[span, :]
+            now = jnp.maximum(was, s)
+            a = jnp.exp(was - now)
+            b = jnp.exp(s - now)
+            whole = total[span, :] * a + b
+            results.append(((mixed[span, :] * a + b * value) / whole).astype(BF16))
+        for span, result in zip(spans, results):
+            out_ref[span, :] = result
         return carry
 
     lax.fori_loop(0, rows // many, finish, 0)

time: 41.6 us -> 41.6 us (level)
  no operation moved by 1% of the time
where the time goes in v3:
time: 41.6 us; the launch traced here: 41.4 us
  Pallas kernels  40.8 us (98%)
  between operations  0.64 us (2%)
    pallas_call x1, Pallas kernels, per_device(): pl.pallas_call(functools.partial(kernel, n), out_shape=(jax.ShapeDtypeStr...  38.9 us
    pallas_call x1, Pallas kernels, per_device(): pl.pallas_call(land, out_shape=(jax.ShapeDtypeStruct(out.shape, BF16), ja...  1.88 us

profile of v3, /device:TPU:0, one launch (start us, length us, event | category | flops | bytes accessed | tf_op | source)
XLA Modules:
  0.0 41.4 jit_solution(7354354914702027544)
XLA Ops:
  0.6 38.9 %shard_map.104 = (bf16[2048,128]{1,0:T(8,128)(2,1)}, bf16[256,128]{1,0:T(8,128)(2,1)}) custom-call(bf16[64,4096]{1,0:T(8,128)(2,1)} %hid_ref.1, s32[1,64]{1,0:T(1,128)} %bitcast.21, s32[8]{0:T(128)} %place_ref.1, s32[64]{0:T(128)} %len_ref.1, bf16[2,64,256]{2,1,0:T(8,128)(2,1)} %bitcast.20, bf16[2048,128]{1,0:T(8,128)(2,1)} %bitcast.19, ...), custom_call_target="tpu_custom_call" | custom-call | tf_op jit(solution)/shard_map/pallas_call | solution.py:361
  39.5 1.9 %shard_map.105 = (bf16[2048,128]{1,0:T(8,128)(2,1)}, bf16[256,128]{1,0:T(8,128)(2,1)}) custom-call(bf16[2048,128]{1,0:T(8,128)(2,1)} %get-tuple-element.6.a_ref, bf16[256,128]{1,0:T(8,128)(2,1)} %get-tuple-element.7.b_ref), custom_call_target="tpu_custom_call" | custom-call | tf_op jit(solution)/shard_map/pallas_call | solution.py:411
